TPU v7x, 256 devices: a whole 4x4x8 slice. The times are simulated.
256 devices in a mesh: dp: 32 (over y, z_hi, x), mp: 8 (over z_lo, core).
Axes of the slice: x: 4, y: 4, z: 8 (z_hi: 2, z_lo: 4; z = z_hi * 4 + z_lo), core: 2. Of those that a mesh axis runs over, the one named last changes fastest.
Arguments:
- tokens: bfloat16 [2048, 6144], P('dp', 'mp'), may hold values from -60 to 60
- norm_gain: float32 [6144], P('mp'), may hold values from 0.5 to 1.5
- w_in: bfloat16 [6144, 24576], P('mp', 'dp'), may hold values from -0.078125 to 0.078125
- b_in: float32 [24576], P('dp'), may hold values from -4 to 4
- w_out: bfloat16 [24576, 6144], P('dp', 'mp'), may hold values from -0.0390625 to 0.0390625
- b_out: float32 [6144], P('mp'), may hold values from -3 to 3
- out_gain: float32 [6144], P('mp'), may hold values from 0.5 to 1.5
- student: bfloat16 [2048, 1024], P(('dp', 'mp')), may hold values from -45 to 45
- w_exit: bfloat16 [1024, 6144], P(None, 'mp'), may hold values from -0.1875 to 0.1875
Outputs:
- mean_loss: float32 [], replicated
- grad_exit: float32 [1024, 6144], P('dp', 'mp')
- grad_student: float32 [2048, 1024], P(('dp', 'mp'))
All inputs are finite; a program needn't handle non-finite values.
Results may differ from a plain program's by a relative error of at most 0.0017.
Values may be sent and summed in bfloat16 or wider, within the bound.
A program may use at most 64 MiB of HBM per device.

v0:
```python
import jax
import jax.numpy as jnp
from jax import lax
from jax.sharding import PartitionSpec as P

epsilon = 1e-06


def shards(tokens, norm_gain, w_in, b_in, w_out, b_out, out_gain, student, w_exit):
    own_rows = tokens.shape[0]
    feature_count = tokens.shape[1] * lax.axis_size("mp")
    total_rows = own_rows * lax.axis_size("dp")
    inputs = tokens.astype(jnp.float32)
    squares = lax.psum(jnp.sum(inputs * inputs, axis=1), "mp")
    scale_in = lax.rsqrt(squares / feature_count + epsilon)
    normed = (inputs * scale_in[:, None] * norm_gain).astype(jnp.bfloat16)
    partial_pre = jnp.dot(
        lax.all_gather(normed, "dp", axis=0, tiled=True), w_in, preferred_element_type=jnp.float32
    )
    preact = lax.psum(partial_pre, "mp") + b_in
    hidden = jax.nn.gelu(preact, approximate=False).astype(jnp.bfloat16)
    rows_now = hidden
    branch = lax.psum_scatter(
        jnp.dot(rows_now, w_out, preferred_element_type=jnp.float32),
        "dp",
        scatter_dimension=0,
        tiled=True,
    )
    features = inputs + branch + b_out
    out_squares = lax.psum(jnp.sum(features * features, axis=1), "mp")
    target = features * lax.rsqrt(out_squares / feature_count + epsilon)[:, None] * out_gain
    learner = lax.all_gather(student, "mp", axis=0, tiled=True)
    predicted = jnp.dot(learner, w_exit, preferred_element_type=jnp.float32)
    errors = predicted - target
    error_sum = lax.psum(jnp.sum(errors * errors), ("dp", "mp"))
    mean_loss = error_sum / (total_rows * feature_count)
    signal = (2.0 * errors).astype(jnp.bfloat16)
    rows_now = signal
    grad_student = lax.psum_scatter(
        lax.dot_general(
            rows_now, w_exit, (((1,), (1,)), ((), ())), preferred_element_type=jnp.float32
        ),
        "mp",
        scatter_dimension=0,
        tiled=True,
    )
    grad_exit = lax.psum_scatter(
        lax.dot_general(
            learner, signal, (((0,), (0,)), ((), ())), preferred_element_type=jnp.float32
        ),
        "dp",
        scatter_dimension=0,
        tiled=True,
    )
    return (mean_loss, grad_exit / total_rows, grad_student)


def solution(mesh):
    placed = (
        P("dp", "mp"),
        P("mp"),
        P("mp", "dp"),
        P("dp"),
        P("dp", "mp"),
        P("mp"),
        P("mp"),
        P(("dp", "mp"), None),
        P(None, "mp"),
    )
    return jax.shard_map(
        shards,
        mesh=mesh,
        in_specs=placed,
        out_specs=(P(), P("dp", "mp"), P(("dp", "mp"), None)),
        check_vma=False,
    )
```

profile of v0, /device:TPU:2, one launch (start us, length us, event | category | flops | bytes accessed | tf_op | source)
XLA Modules:
  0.0 883.0 jit_solution(1066511788309045295)
XLA Ops:
  7.2 1.1 fusion.12
  8.4 17.6 %psum.28 = f32[64]{0:T(128)S(1)} all-reduce(f32[64]{0:T(128)S(1)} %fusion.12), channel_id=1, replica_groups=mesh['dp'=32,'mp'=8] {'mp'}, use_global_device_ids=true, to_apply=%region_1.0 | all-reduce | flops 64 | bytes 512 | tf_op jit(solution)/shard_map/psum | solution.py:14
  26.0 1.6 fusion.14
  27.7 100.5 %all-gather.2.cloned.1.call-done = bf16[2048,768]{1,0:T(8,128)(2,1)} async-done(((bf16[64,768]{1,0:T(8,128)(2,1)}), bf16[2048,768]{1,0:T(8,128)(2,1)}) %all-gather.2.cloned.1.call-update) | async-done | bytes 3145744 | tf_op jit(solution)/shard_map/all_gather | solution.py:18
  128.2 7.5 fusion.49
  135.7 0.0 reduce-scatter.6.cloned.1.call-start
  135.7 143.8 %all-reduce.2.cloned.1.call-done = f32[2048,768]{1,0:T(8,128)} async-done(((f32[2048,768]{1,0:T(8,128)}), f32[2048,768]{1,0:T(8,128)}) %all-reduce.2.cloned.1.call-update) | async-done | bytes 6291472 | tf_op jit(solution)/shard_map/psum | solution.py:20
  279.6 18.8 %fusion.10 = f32[2048,768]{1,0:T(8,128)} fusion(bf16[768,768]{1,0:T(8,128)(2,1)S(1)} %copy-done.5, f32[2048,768]{1,0:T(8,128)} %all-reduce.2.cloned.1.call-done, f32[768]{0:T(1024)S(1)} %copy-done.6), kind=kOutput, calls=%fused_computation.19 | convolution fusion | flops 2519728128 | bytes 13765632 | tf_op jit(solution)/shard_map/dot_general | solution.py:24
  298.4 0.0 reduce-scatter.10.cloned.1.call-start
  298.5 0.6 copy-done.3
  299.1 14.0 %all_gather.6 = bf16[64,1024]{1,0:T(8,128)(2,1)S(1)} all-gather(bf16[8,1024]{1,0:T(8,128)(2,1)S(1)} %copy-done.3), channel_id=1, replica_groups=mesh['dp'=32,'mp'=8] {'mp'}, dimensions={0}, use_global_device_ids=true | all-gather | bytes 147456 | tf_op jit(solution)/shard_map/all_gather | solution.py:32
  313.1 253.0 %reduce-scatter.6.cloned.1.call-done = f32[64,768]{1,0:T(8,128)} async-done(((f32[2048,768]{1,0:T(8,128)}), f32[64,768]{1,0:T(8,128)}) %reduce-scatter.6.cloned.1.call-update) | async-done | bytes 196624 | tf_op jit(solution)/shard_map/reduce_scatter | solution.py:23
  566.1 1.1 multiply_reduce_fusion.1
  567.1 13.6 %psum.30 = f32[64]{0:T(128)S(1)} all-reduce(f32[64]{0:T(128)S(1)} %multiply_reduce_fusion.1), channel_id=1, replica_groups=mesh['dp'=32,'mp'=8] {'mp'}, use_global_device_ids=true, to_apply=%region_5.0 | all-reduce | flops 64 | bytes 512 | tf_op jit(solution)/shard_map/psum | solution.py:30
  580.8 1.9 multiply_reduce_fusion
  582.7 2.3 convolution_bitcast_fusion
  585.0 3.5 copy.14
  588.6 0.0 reduce-scatter.8.cloned.1.call-start
  588.6 1.3 fusion.16
  590.0 73.5 %psum.31 = f32[]{:T(128)} all-reduce(f32[]{:T(128)} %get-tuple-element.9), channel_id=1, replica_groups=mesh['dp'=32,'mp'=8] {'dp','mp'}, use_global_device_ids=true, to_apply=%region_7.0 | all-reduce | flops 1 | bytes 8 | tf_op jit(solution)/shard_map/psum | solution.py:35
  664.1 177.3 %reduce-scatter.10.cloned.1.call-done = f32[32,768]{1,0:T(8,128)} async-done(((f32[1024,768]{1,0:T(8,128)}), f32[32,768]{1,0:T(8,128)}) %reduce-scatter.10.cloned.1.call-update) | async-done | bytes 98320
  841.4 1.1 copy.15
  842.5 0.8 copy.13
  843.3 32.1 %reduce-scatter.8.cloned.1.call-done = f32[8,1024]{1,0:T(8,128)} async-done(((f32[64,1024]{1,0:T(8,128)}), f32[8,1024]{1,0:T(8,128)}) %reduce-scatter.8.cloned.1.call-update) | async-done | bytes 32784 | tf_op jit(solution)/shard_map/reduce_scatter | solution.py:39
  (23 shorter events, 0.2 us)
Async XLA Ops:
  7.2 573.6 %copy-start = (bf16[1024,768]{1,0:T(8,128)(2,1)S(1)}, bf16[1024,768]{1,0:T(8,128)(2,1)}, u32[]{:S(2)}) copy-start(bf16[1024,768]{1,0:T(8,128)(2,1)} %param.17) | copy-start | bytes 4718596
  7.2 121.0 %all-gather.2.cloned.1.call-start = ((), (), s32[]{:S(2)}) async-start(), calls=%async_computation.3 | async-start | bytes 3244032 | tf_op jit(solution)/shard_map/all_gather | solution.py:18
  27.7 251.9 %all-reduce.2.cloned.1.call-start = ((), (), s32[]{:S(2)}) async-start(), calls=%async_computation.4 | async-start | bytes 12582912 | tf_op jit(solution)/shard_map/psum | solution.py:20
  135.7 143.9 %copy-start.5 = (bf16[768,768]{1,0:T(8,128)(2,1)S(1)}, bf16[768,768]{1,0:T(8,128)(2,1)}, u32[]{:S(2)}) copy-start(bf16[768,768]{1,0:T(8,128)(2,1)} %param.13) | copy-start | bytes 3538948
  135.7 143.9 %copy-start.6 = (f32[768]{0:T(1024)S(1)}, f32[768]{0:T(1024)}, u32[]{:S(2)}) copy-start(f32[768]{0:T(1024)} %param.12) | copy-start | bytes 9220
  135.7 430.4 %reduce-scatter.6.cloned.1.call-start = ((), (), s32[]{:S(2)}) async-start(), calls=%async_computation.5 | async-start | bytes 6488064 | tf_op jit(solution)/shard_map/reduce_scatter | solution.py:23
  298.4 0.7 copy-start.3
  298.4 267.7 %copy-start.1 = (bf16[64,768]{1,0:T(8,128)(2,1)S(1)}, bf16[64,768]{1,0:T(8,128)(2,1)}, u32[]{:S(2)}) copy-start(bf16[64,768]{1,0:T(8,128)(2,1)} %param.9) | copy-start | bytes 294916
  298.4 267.7 %copy-start.2 = (f32[768]{0:T(1024)S(1)}, f32[768]{0:T(1024)}, u32[]{:S(2)}) copy-start(f32[768]{0:T(1024)} %param.14) | copy-start | bytes 9220
  298.4 282.4 %copy-start.4 = (f32[768]{0:T(1024)S(1)}, f32[768]{0:T(1024)}, u32[]{:S(2)}) copy-start(f32[768]{0:T(1024)} %param.15) | copy-start | bytes 9220
  298.4 543.0 %reduce-scatter.10.cloned.1.call-start = ((), (), s32[]{:S(2)}) async-start(), calls=%async_computation.7 | async-start | bytes 3244032
  588.6 286.8 %reduce-scatter.8.cloned.1.call-start = ((), (), s32[]{:S(2)}) async-start(), calls=%async_computation.6 | async-start | bytes 294912 | tf_op jit(solution)/shard_map/reduce_scatter | solution.py:39
Sparse Core Ops, SparseCore 0:
  27.8 100.3 all-gather.1
  135.8 143.7 all-reduce.1
  298.5 267.5 reduce-scatter.5
  588.7 252.6 reduce-scatter.9
  844.4 30.8 reduce-scatter.7
where the time goes:
time: 883 us
  waiting for transfers between devices  707 us (80%)
  blocking collectives  119 us (13%)
  matrix products  31.9 us (4%)
  between operations  15.6 us (2%)
    reduce_scatter x1, waiting for transfers between devices, shards(): lax.psum_scatter(jnp.dot(rows_now, w_out, preferred_element_type=jnp.floa...  253 us
    unnamed x6, waiting for transfers between devices  177 us
    psum x1, waiting for transfers between devices, shards(): preact = lax.psum(partial_pre, 'mp') + b_in  144 us
    all_gather x1, waiting for transfers between devices, shards(): lax.all_gather(normed, 'dp', axis=0, tiled=True)  100 us
    psum x1, blocking collectives, shards(): error_sum = lax.psum(jnp.sum(errors * errors), ('dp', 'mp'))  73.5 us
    reduce_scatter x1, waiting for transfers between devices, shards(): lax.psum_scatter(lax.dot_general(rows_now, w_exit, (((1,), (1,)), ((), ()...  32.1 us
    dot_general x1, matrix products, shards(): jnp.dot(rows_now, w_out, preferred_element_type=jnp.float32)  18.8 us
  transfers between devices with their start and end apart: 5, of which 5 were waited for; matrix products, arithmetic and copies ran while one was open for 0% of the time, Pallas kernels for 0%

commit v1 on v0

--- a/solution.py
+++ b/solution.py
@@ -15,7 +15,11 @@
     scale_in = lax.rsqrt(squares / feature_count + epsilon)
     normed = (inputs * scale_in[:, None] * norm_gain).astype(jnp.bfloat16)
     partial_pre = jnp.dot(
-        lax.all_gather(normed, "dp", axis=0, tiled=True), w_in, preferred_element_type=jnp.float32
+        jnp.concatenate(
+            jax.lax.all_to_all(jnp.stack([normed] * jax.lax.axis_size("dp")), "dp", 0, 0), axis=0
+        ),
+        w_in,
+        preferred_element_type=jnp.float32,
     )
     preact = lax.psum(partial_pre, "mp") + b_in
     hidden = jax.nn.gelu(preact, approximate=False).astype(jnp.bfloat16)

time: 883 us -> 864 us (0.978)
  waiting for transfers between devices: 707 us -> 609 us
  blocking collectives: 119 us -> 201 us
    all_gather x1 -> x0, waiting for transfers between devices: 100 us -> none  [shards(): lax.all_gather(normed, 'dp', axis=0, tiled=True)]
    all_to_all x0 -> x1, blocking collectives: none -> 82.2 us  [shards(): jax.lax.all_to_all(jnp.stack([normed] * jax.lax.axis_size('dp')), 'dp', 0...]
    unnamed x6 -> x5, waiting for transfers between devices: 177 us -> 177 us
  transfers between devices with their start and end apart: 5 -> 4, of which waited for: 5 -> 4; matrix products, arithmetic and copies ran while one was open for 0% -> 0% of each run, Pallas kernels for 0% -> 0%
where the time goes in v1:
time: 864 us
  waiting for transfers between devices  609 us (70%)
  blocking collectives  201 us (23%)
  matrix products  28.8 us (3%)
  between operations  15.6 us (2%)
    reduce_scatter x1, waiting for transfers between devices, shards(): lax.psum_scatter(jnp.dot(rows_now, w_out, preferred_element_type=jnp.floa...  253 us
    unnamed x5, waiting for transfers between devices  177 us
    psum x1, waiting for transfers between devices, shards(): preact = lax.psum(partial_pre, 'mp') + b_in  146 us
    all_to_all x1, blocking collectives, shards(): jax.lax.all_to_all(jnp.stack([normed] * jax.lax.axis_size('dp')), 'dp', 0...  82.2 us
    psum x1, blocking collectives, shards(): error_sum = lax.psum(jnp.sum(errors * errors), ('dp', 'mp'))  73.5 us
    reduce_scatter x1, waiting for transfers between devices, shards(): lax.psum_scatter(lax.dot_general(rows_now, w_exit, (((1,), (1,)), ((), ()...  32.1 us
    dot_general x1, matrix products, shards(): jnp.dot(rows_now, w_out, preferred_element_type=jnp.float32)  18.8 us
    psum x1, blocking collectives, shards(): squares = lax.psum(jnp.sum(inputs * inputs, axis=1), 'mp')  17.6 us
  transfers between devices with their start and end apart: 4, of which 4 were waited for; matrix products, arithmetic and copies ran while one was open for 0% of the time, Pallas kernels for 0%

profile of v1, /device:TPU:2, one launch (start us, length us, event | category | flops | bytes accessed | tf_op | source)
XLA Modules:
  0.0 863.9 jit_solution(13470432744026913785)
XLA Ops:
  7.2 1.2 fusion.12
  8.4 17.6 %psum.28 = f32[64]{0:T(128)S(1)} all-reduce(f32[64]{0:T(128)S(1)} %fusion.12), channel_id=1, replica_groups=mesh['dp'=32,'mp'=8] {'mp'}, use_global_device_ids=true, to_apply=%region_1.0 | all-reduce | flops 64 | bytes 512 | tf_op jit(solution)/shard_map/psum | solution.py:14
  26.1 1.0 fusion.14
  27.1 0.3 stack.2
  27.4 82.2 %all_to_all.5 = bf16[32,64,768]{2,1,0:T(8,128)(2,1)S(1)} all-to-all(bf16[32,64,768]{2,1,0:T(8,128)(2,1)S(1)} %stack.2), channel_id=1, replica_groups=mesh['dp'=32,'mp'=8] {'dp'}, dimensions={0} | all-to-all | bytes 6291456 | tf_op jit(solution)/shard_map/all_to_all | solution.py:19
  109.6 4.4 fusion.49
  114.1 0.0 reduce-scatter.6.cloned.1.call-start
  114.1 146.4 %all-reduce.2.cloned.1.call-done = f32[2048,768]{1,0:T(8,128)} async-done(((f32[2048,768]{1,0:T(8,128)}), f32[2048,768]{1,0:T(8,128)}) %all-reduce.2.cloned.1.call-update) | async-done | bytes 6291472 | tf_op jit(solution)/shard_map/psum | solution.py:24
  260.5 18.8 %fusion.10 = f32[2048,768]{1,0:T(8,128)} fusion(bf16[768,768]{1,0:T(8,128)(2,1)S(1)} %copy-done.6, f32[2048,768]{1,0:T(8,128)} %all-reduce.2.cloned.1.call-done, f32[768]{0:T(1024)S(1)} %copy-done.7), kind=kOutput, calls=%fused_computation.19 | convolution fusion | flops 2519728128 | bytes 13765632 | tf_op jit(solution)/shard_map/dot_general | solution.py:28
  279.4 0.0 reduce-scatter.10.cloned.1.call-start
  279.4 0.6 copy-done.3
  280.0 14.0 %all_gather.3 = bf16[64,1024]{1,0:T(8,128)(2,1)S(1)} all-gather(bf16[8,1024]{1,0:T(8,128)(2,1)S(1)} %copy-done.3), channel_id=1, replica_groups=mesh['dp'=32,'mp'=8] {'mp'}, dimensions={0}, use_global_device_ids=true | all-gather | bytes 147456 | tf_op jit(solution)/shard_map/all_gather | solution.py:36
  294.0 252.9 %reduce-scatter.6.cloned.1.call-done = f32[64,768]{1,0:T(8,128)} async-done(((f32[2048,768]{1,0:T(8,128)}), f32[64,768]{1,0:T(8,128)}) %reduce-scatter.6.cloned.1.call-update) | async-done | bytes 196624 | tf_op jit(solution)/shard_map/reduce_scatter | solution.py:27
  546.9 1.1 multiply_reduce_fusion.1
  548.0 13.6 %psum.30 = f32[64]{0:T(128)S(1)} all-reduce(f32[64]{0:T(128)S(1)} %multiply_reduce_fusion.1), channel_id=1, replica_groups=mesh['dp'=32,'mp'=8] {'mp'}, use_global_device_ids=true, to_apply=%region_5.0 | all-reduce | flops 64 | bytes 512 | tf_op jit(solution)/shard_map/psum | solution.py:34
  561.6 1.9 multiply_reduce_fusion
  563.5 2.3 convolution_bitcast_fusion
  565.8 3.5 copy.14
  569.4 1.3 fusion.16
  570.8 73.5 %psum.31 = f32[]{:T(128)} all-reduce(f32[]{:T(128)} %get-tuple-element.9), channel_id=1, replica_groups=mesh['dp'=32,'mp'=8] {'dp','mp'}, use_global_device_ids=true, to_apply=%region_7.0 | all-reduce | flops 1 | bytes 8 | tf_op jit(solution)/shard_map/psum | solution.py:39
  644.9 177.4 %reduce-scatter.10.cloned.1.call-done = f32[32,768]{1,0:T(8,128)} async-done(((f32[1024,768]{1,0:T(8,128)}), f32[32,768]{1,0:T(8,128)}) %reduce-scatter.10.cloned.1.call-update) | async-done | bytes 98320
  822.3 1.1 copy.15
  823.4 0.8 copy.13
  824.2 32.1 %reduce-scatter.8.cloned.1.call-done = f32[8,1024]{1,0:T(8,128)} async-done(((f32[64,1024]{1,0:T(8,128)}), f32[8,1024]{1,0:T(8,128)}) %reduce-scatter.8.cloned.1.call-update) | async-done | bytes 32784 | tf_op jit(solution)/shard_map/reduce_scatter | solution.py:43
  (24 shorter events, 0.2 us)
Async XLA Ops:
  7.2 554.4 %copy-start = (bf16[1024,768]{1,0:T(8,128)(2,1)S(1)}, bf16[1024,768]{1,0:T(8,128)(2,1)}, u32[]{:S(2)}) copy-start(bf16[1024,768]{1,0:T(8,128)(2,1)} %param.17) | copy-start | bytes 4718596
  7.2 102.4 %copy-start.5 = (bf16[768,768]{1,0:T(8,128)(2,1)S(1)}, bf16[768,768]{1,0:T(8,128)(2,1)}, u32[]{:S(2)}) copy-start(bf16[768,768]{1,0:T(8,128)(2,1)} %param.11) | copy-start | bytes 3538948
  7.2 253.3 %all-reduce.2.cloned.1.call-start = ((), (), s32[]{:S(2)}) async-start(), calls=%async_computation.4 | async-start | bytes 12582912 | tf_op jit(solution)/shard_map/psum | solution.py:24
  114.1 146.5 %copy-start.6 = (bf16[768,768]{1,0:T(8,128)(2,1)S(1)}, bf16[768,768]{1,0:T(8,128)(2,1)}, u32[]{:S(2)}) copy-start(bf16[768,768]{1,0:T(8,128)(2,1)} %param.13) | copy-start | bytes 3538948
  114.1 146.5 %copy-start.7 = (f32[768]{0:T(1024)S(1)}, f32[768]{0:T(1024)}, u32[]{:S(2)}) copy-start(f32[768]{0:T(1024)} %param.12) | copy-start | bytes 9220
  114.1 432.8 %reduce-scatter.6.cloned.1.call-start = ((), (), s32[]{:S(2)}) async-start(), calls=%async_computation.5 | async-start | bytes 6488064 | tf_op jit(solution)/shard_map/reduce_scatter | solution.py:27
  279.3 0.7 copy-start.3
  279.3 267.6 %copy-start.1 = (bf16[64,768]{1,0:T(8,128)(2,1)S(1)}, bf16[64,768]{1,0:T(8,128)(2,1)}, u32[]{:S(2)}) copy-start(bf16[64,768]{1,0:T(8,128)(2,1)} %param.9) | copy-start | bytes 294916
  279.3 267.6 %copy-start.2 = (f32[768]{0:T(1024)S(1)}, f32[768]{0:T(1024)}, u32[]{:S(2)}) copy-start(f32[768]{0:T(1024)} %param.14) | copy-start | bytes 9220
  279.3 282.2 %copy-start.4 = (f32[768]{0:T(1024)S(1)}, f32[768]{0:T(1024)}, u32[]{:S(2)}) copy-start(f32[768]{0:T(1024)} %param.15) | copy-start | bytes 9220
  279.4 542.9 %reduce-scatter.10.cloned.1.call-start = ((), (), s32[]{:S(2)}) async-start(), calls=%async_computation.7 | async-start | bytes 3244032
  569.4 286.8 %reduce-scatter.8.cloned.1.call-start = ((), (), s32[]{:S(2)}) async-start(), calls=%async_computation.6 | async-start | bytes 294912 | tf_op jit(solution)/shard_map/reduce_scatter | solution.py:43
Sparse Core Ops, SparseCore 0:
  114.2 146.2 all-reduce.1
  279.5 267.3 reduce-scatter.5
  569.5 252.7 reduce-scatter.9
  825.4 30.8 reduce-scatter.7
